TPU v7x, 32 devices: a whole 2x2x4 slice. The times are simulated.
32 devices in a mesh: outer: 4 (over y, x), inner: 8 (over z, core).
Axes of the slice: x: 2, y: 2, z: 4, core: 2. Of those that a mesh axis runs over, the one named last changes fastest.
Arguments:
- queries: bfloat16 [49152, 2048], P(('outer', 'inner')), may hold values from -6 to 6
- keys: bfloat16 [49152, 2048], P(('outer', 'inner')), may hold values from -6 to 6
- values: bfloat16 [49152, 2048], P(('outer', 'inner')), may hold values from -6 to 6
- gain: float32 [2048], replicated, may hold values from 0.5 to 1.5
- tile_doc: int32 [384], P(('outer', 'inner')), may hold values from 0 to 7, as said below
- tile_fill: int32 [384], P(('outer', 'inner')), may hold values from 1 to 128, as said below
Outputs:
- attended: bfloat16 [49152, 2048], P(('outer', 'inner'))
Inputs may be any that keep to these rules, and one draw needn't show every extreme that they name: tile_doc is 0 at the first tile and rises by 0 or 1 from each tile to the next, so each document holds whole consecutive tiles; the window holds exactly 8 documents. tile_fill is 128 on every tile except the last tile of each document.
All inputs are finite; a program needn't handle non-finite values.
Results may differ from a plain program's by a relative error of at most 0.0027.
Values sent between devices are 32-bit elements; how exact they have to be, the bound alone decides.
A program may use at most 192 MiB of HBM per device.

v0:
```python
from functools import reduce
import jax
import jax.numpy as jnp
from jax import lax
from jax.sharding import PartitionSpec as P

HEADS = 16
HEAD = 128
TILE = 128
BLOCK = 512


def shifted(value, axis, by):
    length = lax.axis_size(axis)
    pairs = [(i, i + by) for i in range(length) if 0 <= i + by < length]
    return lax.ppermute(value, axis, pairs)


def entering(value, axis, join, neutral):
    count, mine = (lax.axis_size(axis), lax.axis_index(axis))
    pieces = jax.tree.map(lambda part: lax.all_gather(part, axis), value)
    so_far = jax.tree.map(
        lambda part, zero: jnp.full_like(part, 0) + jnp.asarray(zero, part.dtype), value, neutral
    )

    def lap(position, so_far):
        longer = join(so_far, jax.tree.map(lambda part: part[position], pieces))
        return jax.tree.map(lambda new, old: jnp.where(position < mine, new, old), longer, so_far)

    return lax.fori_loop(0, count - 1, lap, so_far)


def spread(value, axis, source):
    kept = jnp.where(lax.axis_index(axis) == source, value, 0).astype(value.dtype)
    return lax.psum(kept, axis)


def combine(first, second):
    first_state, first_last, first_single = first
    second_state, second_last, second_single = second
    second_none = second_last[0] == 0
    first_none = first_last[0] == 0
    keep = jnp.logical_or(
        second_none, jnp.logical_and(second_single[0] == 1, second_last[0] == first_last[0])
    )
    state = jnp.where(keep, second_state + first_state, second_state)
    last = jnp.where(second_none, first_last, second_last)
    same = (first_last == second_last).astype(jnp.int32)
    single = jnp.where(
        second_none,
        first_single,
        jnp.where(first_none, second_single, first_single * second_single * same),
    )
    return (state, last, single)


def summarize(key_rows, value_rows, docs, real):
    last_doc = docs[-1]
    chosen = jnp.logical_and(docs == last_doc, real)
    masked = jnp.where(chosen[:, None, None], key_rows, jnp.zeros_like(key_rows))
    state = jnp.einsum("thd,the->hde", masked, value_rows, preferred_element_type=jnp.float32)
    last = (last_doc + 1).reshape(1)
    single = (docs[0] == last_doc).astype(jnp.int32).reshape(1)
    return (state, last, single)


def direct_part(query_rows, key_rows, value_rows, docs, real):
    length = query_rows.shape[0]
    scores = jnp.einsum("qhd,khd->hqk", query_rows, key_rows, preferred_element_type=jnp.float32)
    places = jnp.arange(length)
    allowed = (
        (places[:, None] >= places[None, :]) & (docs[:, None] == docs[None, :]) & real[None, :]
    )
    weights = jnp.where(allowed[None], scores, 0.0).astype(jnp.bfloat16)
    return jnp.einsum("hqk,khd->qhd", weights, value_rows, preferred_element_type=jnp.float32)


def finish(direct, query_rows, docs, real, carry, gain):
    state, last, single = carry
    carried = jnp.einsum(
        "qhd,hde->qhe", query_rows.astype(jnp.float32), state, precision=lax.Precision.HIGHEST
    )
    uses = docs + 1 == last[0]
    raw = direct + jnp.where(uses[:, None, None], carried, 0.0)
    raw = jnp.where(real[:, None, None], raw, 0.0)
    meansq = jnp.mean(raw * raw, axis=-1, keepdims=True)
    normed = raw * lax.rsqrt(meansq + 1e-06) * gain.reshape(HEADS, HEAD)
    return normed.astype(jnp.bfloat16).reshape(query_rows.shape[0], HEADS * HEAD)


def empty_state():
    return (
        jnp.zeros((HEADS, HEAD, HEAD), jnp.float32),
        jnp.zeros((1,), jnp.int32),
        jnp.zeros((1,), jnp.int32),
    )


def across_groups(total):
    earlier = empty_state()
    for step in range(lax.axis_size("outer") - 1):
        running = combine(earlier, total)
        earlier = shifted((running[0], running[1], running[2]), "outer", 1)
    return earlier


def body(queries, keys, values, gain, tile_doc, tile_fill):
    length = queries.shape[0]
    count = length // BLOCK
    docs = jnp.repeat(tile_doc, TILE)
    real = jnp.arange(length, dtype=jnp.int32) % TILE < jnp.repeat(tile_fill, TILE)
    query_all = queries.reshape(length, HEADS, HEAD)
    key_all = keys.reshape(length, HEADS, HEAD)
    value_all = values.reshape(length, HEADS, HEAD)
    directs = []
    summaries = []
    for block in range(count):
        lower = block * BLOCK
        upper = lower + BLOCK
        directs.append(
            direct_part(
                query_all[lower:upper],
                key_all[lower:upper],
                value_all[lower:upper],
                docs[lower:upper],
                real[lower:upper],
            )
        )
        summaries.append(
            summarize(
                key_all[lower:upper], value_all[lower:upper], docs[lower:upper], real[lower:upper]
            )
        )
    own = reduce(combine, summaries)
    before_inner = entering(own, "inner", combine, empty_state())
    through = combine(before_inner, own)
    total = (
        spread(through[0], "inner", lax.axis_size("inner") - 1),
        spread(through[1], "inner", lax.axis_size("inner") - 1),
        spread(through[2], "inner", lax.axis_size("inner") - 1),
    )
    prefix = combine(across_groups(total), before_inner)
    carry = prefix
    results = []
    for block in range(count):
        lower = block * BLOCK
        upper = lower + BLOCK
        results.append(
            finish(
                directs[block],
                query_all[lower:upper],
                docs[lower:upper],
                real[lower:upper],
                carry,
                gain,
            )
        )
        carry = combine(carry, summaries[block])
    return jnp.concatenate(results, axis=0)


def solution(mesh):
    placed = (
        P(("outer", "inner"), None),
        P(("outer", "inner"), None),
        P(("outer", "inner"), None),
        P(),
        P(("outer", "inner")),
        P(("outer", "inner")),
    )
    return jax.shard_map(
        body, mesh=mesh, in_specs=placed, out_specs=P(("outer", "inner"), None), check_vma=False
    )
```

profile of v0, /device:TPU:4, one launch (start us, length us, event | category | flops | bytes accessed | tf_op | source)
XLA Modules:
  0.0 397.3 jit_solution(3273020750897445659)
XLA Ops:
  6.5 0.8 fusion.58
  13.7 0.7 fusion.30
  14.4 1.8 fusion.54
  16.3 5.9 %fusion.52 = (bf16[512,2048]{1,0:T(8,128)(2,1)}, bf16[512,2048]{1,0:T(8,128)(2,1)S(1)}, bf16[512,2048]{1,0:T(8,128)(2,1)}) fusion(bf16[1536,2048]{1,0:T(8,128)(2,1)} %param.9), kind=kLoop, calls=%fused_computation.91 | loop fusion | bytes 12582912 | tf_op jit(solution)/shard_map/slice | solution.py:123
  22.1 3.9 copy.108
  26.1 5.8 %fusion.53 = (bf16[512,2048]{1,0:T(8,128)(2,1)}, bf16[512,2048]{1,0:T(8,128)(2,1)}, bf16[512,2048]{1,0:T(8,128)(2,1)}) fusion(bf16[1536,2048]{1,0:T(8,128)(2,1)} %param.10), kind=kLoop, calls=%fused_computation.92 | loop fusion | bytes 12582912 | tf_op jit(solution)/shard_map/slice | solution.py:124
  31.9 4.0 copy.69
  35.8 3.9 copy.111
  39.8 3.9 copy.112
  43.7 2.5 copy.109
  46.2 4.1 %copy.110 = bf16[512,2048]{0,1:T(8,128)(2,1)} copy(bf16[512,2048]{1,0:T(8,128)(2,1)} %get-tuple-element.205) | data formatting | bytes 4194304
  50.2 2.4 fusion.7
  53.1 0.7 fusion.9
  53.8 0.9 copy-done.9
  54.7 1.0 copy-done.10
  55.7 1.7 add_select_fusion.7
  60.0 1.3 dynamic-update-slice.1
  61.3 0.7 dynamic-update-slice
  62.0 9.3 %all-reduce.3 = (s32[8]{0:T(128)S(1)}, s32[8]{0:T(128)S(1)}) all-reduce(s32[8]{0:T(128)S(1)} %dynamic-update-slice, s32[8]{0:T(128)S(1)} %dynamic-update-slice.1), channel_id=2, replica_groups=mesh['outer'=4,'inner'=8] {'inner'}, use_global_device_ids=true, to_apply=%add | all-reduce | flops 16 | bytes 128
  71.3 69.7 %all-gather.5.cloned.1.call-done = f32[128,128,128]{2,1,0:T(8,128)} async-done(((f32[16,128,128]{2,1,0:T(8,128)}), f32[128,128,128]{2,1,0:T(8,128)}) %all-gather.5.cloned.1.call-update) | async-done | bytes 8388624 | tf_op jit(solution)/shard_map/all_gather | solution.py:21
  141.0 54.9 %while.18 = (s32[]{:T(128)}, f32[16,128,128]{2,1,0:T(8,128)S(1)}, s32[1]{0:T(128)}, s32[1]{0:T(128)}, s32[]{:T(128)}, /*index=5*/s32[8,1]{0,1:T(1,128)S(1)}, s32...) while((s32[]{:T(128)}, f32[16,128,128]{2,1,0:T(8,128)S(1)}, ...), condition=%wide.region_1.2_spmd.clone, body=%wide.region_0.1_spmd.clone.sunk | while | flops 1048594 | bytes 3146019 | solution.py:30
  142.3 0.7 fusion.78
  146.4 1.7 fusion.79
  148.8 0.7 constant_dynamic-slice_fusion.3
  150.2 0.7 fusion.78
  154.2 1.7 fusion.79
  162.1 1.7 fusion.79
  169.9 1.7 fusion.79
  177.8 1.7 fusion.79
  185.6 1.7 fusion.79
  193.5 1.7 fusion.79
  196.5 1.1 fusion.18
  197.7 57.4 %all-reduce.6.cloned.1.call-done = f32[16,128,128]{2,1,0:T(8,128)} async-done(((f32[16,128,128]{2,1,0:T(8,128)}), f32[16,128,128]{2,1,0:T(8,128)}) %all-reduce.6.cloned.1.call-update) | async-done | bytes 1048592 | tf_op jit(solution)/shard_map/psum | solution.py:35
  255.0 3.4 collective-permute-start.3
  258.4 1.1 fusion.26
  259.5 5.7 %fusion.51 = (bf16[512,2048]{1,0:T(8,128)(2,1)}, bf16[512,2048]{1,0:T(8,128)(2,1)}, bf16[512,2048]{1,0:T(8,128)(2,1)}) fusion(bf16[1536,2048]{1,0:T(8,128)(2,1)} %param.8), kind=kLoop, calls=%fused_computation.90 | loop fusion | bytes 12582912 | tf_op jit(solution)/shard_map/slice | solution.py:122
  266.5 2.9 copy.114
  269.4 7.8 %all-reduce.2 = (s32[1]{0:T(128)}, s32[1]{0:T(128)}) all-reduce(s32[1]{0:T(128)S(6)} %select_n.305, s32[1]{0:T(128)S(6)} %select_n.313), channel_id=1, replica_groups=mesh['outer'=4,'inner'=8] {'inner'}, use_global_device_ids=true, to_apply=%region_2.3 | all-reduce | flops 2 | bytes 16 | tf_op jit(solution)/shard_map/psum | solution.py:35
  278.3 3.2 collective-permute-start
  282.1 2.5 collective-permute-done
  285.9 2.8 add_select_fusion.5
  288.6 2.1 collective-permute-start.4
  290.7 9.4 %fusion.6 = f32[16,512,128]{1,2,0:T(8,128)} fusion(bf16[512,16,128]{0,2,1:T(8,128)(2,1)} %bitcast.158, bf16[512,16,128]{0,2,1:T(8,128)(2,1)S(1)} %bitcast.138, bf16[512,16,128]{0,2,1:T(8,128)(2,1)} %bitcast.156, pred[512,512]{1,0:T(8,128)(4,1)} %get-tuple-element.236), kind=kOutput, calls=%fused_computation.22 | convolution fusion | flops 2155872256 | bytes 10747904 | tf_op jit(solution)/shard_map/hqk,khd->qhd/dot_general | solution.py:75
  300.1 3.9 copy.113
  304.0 3.9 copy.107
  307.9 0.9 fusion.25
  308.8 10.0 %fusion.5 = f32[16,512,128]{1,2,0:T(8,128)} fusion(bf16[512,16,128]{0,2,1:T(8,128)(2,1)} %bitcast.154, bf16[512,16,128]{0,2,1:T(8,128)(2,1)} %bitcast.142, bf16[512,16,128]{0,2,1:T(8,128)(2,1)} %bitcast.152, pred[512,512]{1,0:T(8,128)(4,1)S(1)} %get-tuple-element.235), kind=kOutput, calls=%fused_computation.21 | convolution fusion | flops 2155872256 | bytes 10747904 | tf_op jit(solution)/shard_map/hqk,khd->qhd/dot_general | solution.py:75
  320.1 3.2 collective-permute-start.1
  323.3 3.1 collective-permute-done.1
  327.7 2.6 add_select_fusion.4
  330.4 1.9 collective-permute-start.5
  332.3 10.0 %fusion.4 = f32[16,512,128]{1,2,0:T(8,128)} fusion(bf16[512,16,128]{0,2,1:T(8,128)(2,1)} %bitcast.151, bf16[512,16,128]{0,2,1:T(8,128)(2,1)} %bitcast.140, bf16[512,16,128]{0,2,1:T(8,128)(2,1)} %bitcast.148, pred[512,512]{1,0:T(8,128)(4,1)S(1)} %copy-done.13), kind=kOutput, calls=%fused_computation.20 | convolution fusion | flops 2155872256 | bytes 10747904 | tf_op jit(solution)/shard_map/hqk,khd->qhd/dot_general | solution.py:75
  343.5 8.7 %collective-permute-start.2 = (s32[1]{0:T(128)}, s32[1]{0:T(128)}, u32[]{:S(2)}, u32[]{:S(2)}) collective-permute-start(s32[1]{0:T(128)} %select_n.308), channel_id=1, source_target_pairs={{0,8},{8,16},{16,24},{1,9},{9,17},{17,25},{2,10},{10,18},{18,26},{... | collective-permute-start | bytes 20 | tf_op jit(solution)/shard_map/ppermute | solution.py:16
  352.2 3.1 collective-permute-done.2
  356.9 1.9 add_select_fusion.2
  358.8 0.9 copy-done.4
  359.7 4.1 %multiply_reduce_fusion = (f32[512,16]{0,1:T(8,128)S(1)}, f32[512,16,128]{0,2,1:T(8,128)S(1)}) fusion(bf16[512,16,128]{0,2,1:T(8,128)(2,1)S(1)} %bitcast.139, f32[16,128,128]{2,1,0:T(8,128)} %copy-done.11, f32[16,128,128]{2,1,0:T(8,128)S(1)} %add_select_fusion.2, pred[]{:T(512)S(6)} %or.55, pred[512]{0:T(512)(128)(4,1)S(1)} %get-tuple-element.234, ...), kind=kOutput, calls=%fused_computation.15 | convolution fusion | flops 1616371712 | bytes 12616705 | tf_op jit(solution)/shard_map/qhd,hde->qhe/dot_general | solution.py:80
  363.8 2.6 multiply_reduce_fusion.1
  366.7 4.0 multiply_reduce_fusion.2
  370.7 3.6 multiply_convert_fusion.2
  374.3 2.9 copy.89
  377.2 4.0 copy.90
  381.1 4.0 copy.91
  385.1 5.4 %pad_maximum_fusion = bf16[1536,2048]{1,0:T(8,128)(2,1)} fusion(bf16[512,2048]{1,0:T(8,128)(2,1)} %copy.91, bf16[512,2048]{1,0:T(8,128)(2,1)} %copy.90, bf16[512,2048]{1,0:T(8,128)(2,1)S(1)} %copy.89), kind=kLoop, calls=%fused_computation.7 | loop fusion | flops 18874368 | bytes 12582912 | tf_op jit(solution)/shard_map/concatenate | solution.py:159
  (63 shorter events, 11.4 us)
Async XLA Ops:
  6.5 134.4 %all-gather.5.cloned.1.call-start = ((), (), s32[]{:S(2)}) async-start(), calls=%async_computation.1 | async-start | bytes 9437184 | tf_op jit(solution)/shard_map/all_gather | solution.py:21
  46.2 4.1 %copy-start.6 = (bf16[512,2048]{0,1:T(8,128)(2,1)S(1)}, bf16[512,2048]{0,1:T(8,128)(2,1)}, u32[]{:S(2)}) copy-start(bf16[512,2048]{0,1:T(8,128)(2,1)} %copy.108) | copy-start | bytes 6291460
  50.2 2.5 copy-start.7
  50.2 2.9 copy-start.8
  52.7 1.1 copy-start.12
  53.1 1.6 copy-start.9
  53.1 2.6 copy-start.10
  53.8 3.6 copy-start.11
  55.7 3.1 copy-start.15
  57.5 197.6 %all-reduce.6.cloned.1.call-start = ((), (), s32[]{:S(2)}) async-start(), calls=%async_computation | async-start | bytes 2097152 | tf_op jit(solution)/shard_map/psum | solution.py:35
  141.0 55.5 %copy-start.5 = (f32[16,128,128]{2,1,0:T(8,128)S(1)}, f32[16,128,128]{2,1,0:T(8,128)}, u32[]{:S(2)}) copy-start(f32[16,128,128]{2,1,0:T(8,128)} %add_select_fusion.7) | copy-start | bytes 3145732
  255.0 30.8 %collective-permute-start.3 = (f32[16,128,128]{2,1,0:T(8,128)}, f32[16,128,128]{2,1,0:T(8,128)}, u32[]{:S(2)}, u32[]{:S(2)}) collective-permute-start(f32[16,128,128]{2,1,0:T(8,128)} %all-reduce.6.cloned.1.call-done), channel_id=1, source_target_pairs={{0,8},{8,16},{16,24},{1,9},{9,17},{17,25},{2,10},{10,18},{18,26},{... | collective-permute-start | bytes 3145736 | tf_op jit(solution)/shard_map/ppermute | solution.py:16
  278.3 6.3 %collective-permute-start = (s32[1]{0:T(128)}, s32[1]{0:T(128)}, u32[]{:S(2)}, u32[]{:S(2)}) collective-permute-start(s32[1]{0:T(128)} %select_n.306), channel_id=1, source_target_pairs={{0,8},{8,16},{16,24},{1,9},{9,17},{17,25},{2,10},{10,18},{18,26},{... | collective-permute-start | bytes 20 | tf_op jit(solution)/shard_map/ppermute | solution.py:16
  288.6 39.1 %collective-permute-start.4 = (f32[16,128,128]{2,1,0:T(8,128)}, f32[16,128,128]{2,1,0:T(8,128)}, u32[]{:S(2)}, u32[]{:S(2)}) collective-permute-start(f32[16,128,128]{2,1,0:T(8,128)} %add_select_fusion.5), channel_id=1, source_target_pairs={{0,8},{8,16},{16,24},{1,9},{9,17},{17,25},{2,10},{10,18},{18,26},{... | collective-permute-start | bytes 3145736 | tf_op jit(solution)/shard_map/ppermute | solution.py:16
  318.8 13.5 %copy-start.13 = (pred[512,512]{1,0:T(8,128)(4,1)S(1)}, pred[512,512]{1,0:T(8,128)(4,1)}, u32[]{:S(2)}) copy-start(pred[512,512]{1,0:T(8,128)(4,1)} %fusion.25) | copy-start | bytes 786436
  320.1 6.3 %collective-permute-start.1 = (s32[1]{0:T(128)}, s32[1]{0:T(128)}, u32[]{:S(2)}, u32[]{:S(2)}) collective-permute-start(s32[1]{0:T(128)} %select_n.307), channel_id=1, source_target_pairs={{0,8},{8,16},{16,24},{1,9},{9,17},{17,25},{2,10},{10,18},{18,26},{... | collective-permute-start | bytes 20 | tf_op jit(solution)/shard_map/ppermute | solution.py:16
  330.4 26.5 %collective-permute-start.5 = (f32[16,128,128]{2,1,0:T(8,128)}, f32[16,128,128]{2,1,0:T(8,128)}, u32[]{:S(2)}, u32[]{:S(2)}) collective-permute-start(f32[16,128,128]{2,1,0:T(8,128)} %add_select_fusion.4), channel_id=1, source_target_pairs={{0,8},{8,16},{16,24},{1,9},{9,17},{17,25},{2,10},{10,18},{18,26},{... | collective-permute-start | bytes 3145736 | tf_op jit(solution)/shard_map/ppermute | solution.py:16
  343.5 11.8 %collective-permute-start.2 = (s32[1]{0:T(128)}, s32[1]{0:T(128)}, u32[]{:S(2)}, u32[]{:S(2)}) collective-permute-start(s32[1]{0:T(128)} %select_n.308), channel_id=1, source_target_pairs={{0,8},{8,16},{16,24},{1,9},{9,17},{17,25},{2,10},{10,18},{18,26},{... | collective-permute-start | bytes 20 | tf_op jit(solution)/shard_map/ppermute | solution.py:16
  356.9 2.8 copy-start.4
  359.7 4.1 %copy-start.2 = (bf16[512,2048]{0,1:T(8,128)(2,1)S(1)}, bf16[512,2048]{0,1:T(8,128)(2,1)}, u32[]{:S(2)}) copy-start(bf16[512,2048]{0,1:T(8,128)(2,1)} %copy.113) | copy-start | bytes 6291460
  359.7 4.1 %copy-start.3 = (f32[16,512,128]{1,2,0:T(8,128)S(1)}, f32[16,512,128]{1,2,0:T(8,128)}, u32[]{:S(2)}) copy-start(f32[16,512,128]{1,2,0:T(8,128)} %fusion.5) | copy-start | bytes 12582916
  363.8 2.6 copy-start
  363.8 2.9 copy-start.1
  366.7 4.0 %copy-start.14 = (f32[2048]{0:T(1024)S(1)}, f32[2048]{0:T(1024)}, u32[]{:S(2)}) copy-start(f32[2048]{0:T(1024)} %param.11) | copy-start | bytes 24580
Sparse Core Ops, SparseCore 0:
  57.6 83.3 all-gather.4
  197.8 57.2 all-reduce.5
where the time goes:
time: 399 us; the launch traced here: 397 us
  waiting for transfers between devices  136 us (34%)
  local copies, waits for them, and re-layouts  74.8 us (19%)
  matrix products  44.8 us (11%)
  other arithmetic  39.6 us (10%)
  loops' own time  33.4 us (8%)
  between operations  29.4 us (7%)
  starting transfers between devices  22.5 us (6%)
  blocking collectives  17.1 us (4%)
    all_gather x1, waiting for transfers between devices, entering(): pieces = jax.tree.map(lambda part: lax.all_gather(part, axis), value)  69.7 us
    psum x1, waiting for transfers between devices, spread(): return lax.psum(kept, axis)  57.4 us
    unnamed x45, local copies, waits for them, and re-layouts  35.1 us
    another operation x1, loops' own time, entering(): return lax.fori_loop(0, count - 1, lap, so_far)  33.4 us
    dot_general x3, matrix products, direct_part(): jnp.einsum('hqk,khd->qhd', weights, value_rows, preferred_element_type=jn...  29.3 us
    ppermute x6, starting transfers between devices, shifted(): return lax.ppermute(value, axis, pairs)  22.5 us
    select_n x7, other arithmetic, lap(): jnp.where(position < mine, new, old)  12.2 us
    reshape x3, local copies, waits for them, and re-layouts, finish(): normed.astype(jnp.bfloat16).reshape(query_rows.shape[0], HEADS * HEAD)  10.8 us
  transfers between devices with their start and end apart: 8, of which 5 were waited for; matrix products, arithmetic and copies ran while one was open for 13% of the time, Pallas kernels for 0%

commit v1 on v0

--- a/solution.py
+++ b/solution.py
@@ -32,7 +32,7 @@
 
 def spread(value, axis, source):
     kept = jnp.where(lax.axis_index(axis) == source, value, 0).astype(value.dtype)
-    return lax.psum(kept, axis)
+    return jnp.sum(lax.all_gather(kept, axis), axis=0)
 
 
 def combine(first, second):

time: 399 us -> 422 us (1.058)
  waiting for transfers between devices: 136 us -> 159 us
  other arithmetic: 39.6 us -> 46.2 us
    all_gather x0 -> x1, waiting for transfers between devices: none -> 80.7 us  [spread(): return jnp.sum(lax.all_gather(kept, axis), axis=0)]
    psum x1 -> x0, waiting for transfers between devices: 57.4 us -> none  [spread(): return lax.psum(kept, axis)]
    psum x1 -> x0, blocking collectives: 7.79 us -> none  [spread(): return lax.psum(kept, axis)]
    unnamed x1 -> x2, blocking collectives: 9.27 us -> 16 us
    reduce_sum x0 -> x3, other arithmetic: none -> 5.5 us  [spread(): return jnp.sum(lax.all_gather(kept, axis), axis=0)]
where the time goes in v1:
time: 422 us; the launch traced here: 420 us
  waiting for transfers between devices  159 us (38%)
  local copies, waits for them, and re-layouts  74.3 us (18%)
  other arithmetic  46.2 us (11%)
  matrix products  45 us (11%)
  loops' own time  29.5 us (7%)
  between operations  27.9 us (7%)
  starting transfers between devices  22.2 us (5%)
  blocking collectives  16 us (4%)
    all_gather x1, waiting for transfers between devices, spread(): return jnp.sum(lax.all_gather(kept, axis), axis=0)  80.7 us
    all_gather x1, waiting for transfers between devices, entering(): pieces = jax.tree.map(lambda part: lax.all_gather(part, axis), value)  69.7 us
    unnamed x45, local copies, waits for them, and re-layouts  35.4 us
    dot_general x3, matrix products, direct_part(): jnp.einsum('hqk,khd->qhd', weights, value_rows, preferred_element_type=jn...  29.9 us
    another operation x1, loops' own time, entering(): return lax.fori_loop(0, count - 1, lap, so_far)  29.5 us
    ppermute x6, starting transfers between devices, shifted(): return lax.ppermute(value, axis, pairs)  22.1 us
    unnamed x2, blocking collectives  16 us
    select_n x7, other arithmetic, lap(): jnp.where(position < mine, new, old)  12.2 us
  transfers between devices with their start and end apart: 8, of which 5 were waited for; matrix products, arithmetic and copies ran while one was open for 13% of the time, Pallas kernels for 0%

profile of v1, /device:TPU:4, one launch (start us, length us, event | category | flops | bytes accessed | tf_op | source)
XLA Modules:
  0.0 419.7 jit_solution(13937355104642246741)
XLA Ops:
  6.5 0.8 fusion.60
  13.8 0.7 fusion.30
  14.5 1.9 fusion.56
  16.4 5.8 %fusion.54 = (bf16[512,2048]{1,0:T(8,128)(2,1)}, bf16[512,2048]{1,0:T(8,128)(2,1)S(1)}, bf16[512,2048]{1,0:T(8,128)(2,1)}) fusion(bf16[1536,2048]{1,0:T(8,128)(2,1)} %param.9), kind=kLoop, calls=%fused_computation.96 | loop fusion | bytes 12582912 | tf_op jit(solution)/shard_map/slice | solution.py:123
  22.2 4.0 copy.108
  26.2 5.8 %fusion.55 = (bf16[512,2048]{1,0:T(8,128)(2,1)}, bf16[512,2048]{1,0:T(8,128)(2,1)}, bf16[512,2048]{1,0:T(8,128)(2,1)}) fusion(bf16[1536,2048]{1,0:T(8,128)(2,1)} %param.10), kind=kLoop, calls=%fused_computation.97 | loop fusion | bytes 12582912 | tf_op jit(solution)/shard_map/slice | solution.py:124
  32.0 4.0 copy.69
  35.9 3.9 copy.111
  39.9 3.9 copy.112
  43.8 2.5 copy.109
  46.3 4.1 copy.110
  50.4 2.4 fusion.7
  53.2 0.7 fusion.9
  53.9 0.9 copy-done.9
  55.4 1.8 add_select_fusion.7
  59.7 1.4 dynamic-update-slice.1
  61.0 0.7 dynamic-update-slice
  61.8 9.3 %all-reduce.5 = (s32[8]{0:T(128)S(1)}, s32[8]{0:T(128)S(1)}) all-reduce(s32[8]{0:T(128)S(1)} %dynamic-update-slice, s32[8]{0:T(128)S(1)} %dynamic-update-slice.1), channel_id=2, replica_groups=mesh['outer'=4,'inner'=8] {'inner'}, use_global_device_ids=true, to_apply=%add | all-reduce | flops 16 | bytes 128
  71.0 69.7 %all-gather.9.cloned.1.call-done = f32[128,128,128]{2,1,0:T(8,128)} async-done(((f32[16,128,128]{2,1,0:T(8,128)}), f32[128,128,128]{2,1,0:T(8,128)}) %all-gather.9.cloned.1.call-update) | async-done | bytes 8388624 | tf_op jit(solution)/shard_map/all_gather | solution.py:21
  140.7 50.2 %while.18 = (s32[]{:T(128)}, f32[16,128,128]{2,1,0:T(8,128)S(1)}, s32[1]{0:T(128)}, s32[1]{0:T(128)}, s32[]{:T(128)}, /*index=5*/s32[8,1]{0,1:T(1,128)S(1)}, s32...) while((s32[]{:T(128)}, f32[16,128,128]{2,1,0:T(8,128)S(1)}, ...), condition=%wide.region_1.2_spmd.clone, body=%wide.region_0.1_spmd.clone.sunk | while | flops 1048594 | bytes 3146019 | solution.py:30
  145.6 1.7 fusion.81
  149.0 0.7 fusion.80
  152.8 1.7 fusion.81
  159.9 1.7 fusion.81
  167.1 1.7 fusion.81
  174.3 1.7 fusion.81
  181.5 1.7 fusion.81
  188.6 1.7 fusion.81
  191.5 1.1 fusion.18
  192.7 80.7 %all-gather.11.cloned.1.call-done = f32[128,128,128]{2,1,0:T(8,128)} async-done(((f32[16,128,128]{2,1,0:T(8,128)}), f32[128,128,128]{2,1,0:T(8,128)}) %all-gather.11.cloned.1.call-update) | async-done | bytes 8388624 | tf_op jit(solution)/shard_map/all_gather | solution.py:35
  273.3 4.2 reduce_sum.59
  277.5 3.4 collective-permute-start.3
  280.9 1.1 fusion.26
  282.0 5.7 %fusion.53 = (bf16[512,2048]{1,0:T(8,128)(2,1)}, bf16[512,2048]{1,0:T(8,128)(2,1)}, bf16[512,2048]{1,0:T(8,128)(2,1)}) fusion(bf16[1536,2048]{1,0:T(8,128)(2,1)} %param.8), kind=kLoop, calls=%fused_computation.95 | loop fusion | bytes 12582912 | tf_op jit(solution)/shard_map/slice | solution.py:122
  287.7 0.7 select_dynamic-update-slice_fusion.1
  288.4 1.4 select_dynamic-update-slice_fusion
  289.8 3.9 copy.114
  293.7 6.8 %all-reduce.4 = (s32[8]{0:T(128)S(1)}, s32[8]{0:T(128)S(1)}) all-reduce(s32[8]{0:T(128)S(1)} %select_dynamic-update-slice_fusion.1, s32[8]{0:T(128)S(1)} %select_dynamic-update-slice_fusion), channel_id=5, replica_groups=mesh['outer'=4,'inner'=8] {'inner'}, use_global_device_ids=true, to_apply=%add.2 | all-reduce | flops 16 | bytes 128
  300.5 0.7 reduce.2
  302.4 3.2 collective-permute-start
  306.8 2.0 collective-permute-done
  310.1 2.4 add_select_fusion.5
  312.5 2.1 collective-permute-start.4
  314.6 10.0 %fusion.6 = f32[16,512,128]{1,2,0:T(8,128)} fusion(bf16[512,16,128]{0,2,1:T(8,128)(2,1)} %bitcast.162, bf16[512,16,128]{0,2,1:T(8,128)(2,1)} %bitcast.141, bf16[512,16,128]{0,2,1:T(8,128)(2,1)} %bitcast.160, pred[512,512]{1,0:T(8,128)(4,1)} %get-tuple-element.236), kind=kOutput, calls=%fused_computation.22 | convolution fusion | flops 2155872256 | bytes 10747904 | tf_op jit(solution)/shard_map/hqk,khd->qhd/dot_general | solution.py:75
  324.5 3.9 copy.113
  328.5 3.9 copy.107
  332.4 0.9 fusion.25
  333.3 9.9 %fusion.5 = f32[16,512,128]{1,2,0:T(8,128)} fusion(bf16[512,16,128]{0,2,1:T(8,128)(2,1)} %bitcast.158, bf16[512,16,128]{0,2,1:T(8,128)(2,1)} %bitcast.146, bf16[512,16,128]{0,2,1:T(8,128)(2,1)} %bitcast.156, pred[512,512]{1,0:T(8,128)(4,1)S(1)} %get-tuple-element.235), kind=kOutput, calls=%fused_computation.21 | convolution fusion | flops 2155872256 | bytes 10747904 | tf_op jit(solution)/shard_map/hqk,khd->qhd/dot_general | solution.py:75
  344.5 3.2 collective-permute-start.1
  347.7 3.1 collective-permute-done.1
  352.1 2.4 add_select_fusion.4
  354.5 1.9 collective-permute-start.5
  356.4 10.0 %fusion.4 = f32[16,512,128]{1,2,0:T(8,128)} fusion(bf16[512,16,128]{0,2,1:T(8,128)(2,1)} %bitcast.155, bf16[512,16,128]{0,2,1:T(8,128)(2,1)} %bitcast.143, bf16[512,16,128]{0,2,1:T(8,128)(2,1)} %bitcast.152, pred[512,512]{1,0:T(8,128)(4,1)S(1)} %copy-done.12), kind=kOutput, calls=%fused_computation.20 | convolution fusion | flops 2155872256 | bytes 10747904 | tf_op jit(solution)/shard_map/hqk,khd->qhd/dot_general | solution.py:75
  367.7 8.3 %collective-permute-start.2 = (s32[1]{0:T(128)}, s32[1]{0:T(128)}, u32[]{:S(2)}, u32[]{:S(2)}) collective-permute-start(s32[1]{0:T(128)} %select_n.311), channel_id=1, source_target_pairs={{0,8},{8,16},{16,24},{1,9},{9,17},{17,25},{2,10},{10,18},{18,26},{... | collective-permute-start | bytes 20 | tf_op jit(solution)/shard_map/ppermute | solution.py:16
  376.0 3.1 collective-permute-done.2
  380.5 1.6 add_select_fusion.2
  382.4 4.9 %multiply_reduce_fusion = (f32[512,16]{0,1:T(8,128)S(1)}, f32[512,16,128]{0,2,1:T(8,128)S(1)}) fusion(bf16[512,16,128]{0,2,1:T(8,128)(2,1)S(1)} %bitcast.142, f32[16,128,128]{2,1,0:T(8,128)S(1)} %fusion.9, f32[16,128,128]{2,1,0:T(8,128)S(1)} %add_select_fusion.2, pred[]{:T(512)S(6)} %or.47, pred[512]{0:T(512)(128)(4,1)S(1)} %get-tuple-element.234, ...), kind=kOutput, calls=%fused_computation.15 | convolution fusion | flops 1616371712 | bytes 12616705 | tf_op jit(solution)/shard_map/qhd,hde->qhe/dot_general | solution.py:80
  387.4 2.6 multiply_reduce_fusion.1
  390.3 2.7 multiply_reduce_fusion.2
  393.0 3.6 multiply_convert_fusion.2
  396.6 2.9 copy.89
  399.5 4.0 copy.90
  403.5 4.0 copy.91
  407.5 5.4 %pad_maximum_fusion = bf16[1536,2048]{1,0:T(8,128)(2,1)} fusion(bf16[512,2048]{1,0:T(8,128)(2,1)} %copy.91, bf16[512,2048]{1,0:T(8,128)(2,1)} %copy.90, bf16[512,2048]{1,0:T(8,128)(2,1)S(1)} %copy.89), kind=kLoop, calls=%fused_computation.7 | loop fusion | flops 18874368 | bytes 12582912 | tf_op jit(solution)/shard_map/concatenate | solution.py:159
  (68 shorter events, 13.6 us)
Async XLA Ops:
  6.5 134.2 %all-gather.9.cloned.1.call-start = ((), (), s32[]{:S(2)}) async-start(), calls=%async_computation | async-start | bytes 9437184 | tf_op jit(solution)/shard_map/all_gather | solution.py:21
  46.3 4.1 copy-start.6
  50.4 2.5 copy-start.7
  50.4 2.9 copy-start.8
  52.8 1.1 copy-start.11
  53.2 1.6 copy-start.9
  53.2 2.2 copy-start.10
  55.4 3.0 copy-start.14
  57.2 216.1 %all-gather.11.cloned.1.call-start = ((), (), s32[]{:S(2)}) async-start(), calls=%async_computation.1 | async-start | bytes 9437184 | tf_op jit(solution)/shard_map/all_gather | solution.py:35
  140.7 50.8 %copy-start.5 = (f32[16,128,128]{2,1,0:T(8,128)S(1)}, f32[16,128,128]{2,1,0:T(8,128)}, u32[]{:S(2)}) copy-start(f32[16,128,128]{2,1,0:T(8,128)} %add_select_fusion.7) | copy-start | bytes 3145732
  277.5 32.5 %collective-permute-start.3 = (f32[16,128,128]{2,1,0:T(8,128)S(1)}, f32[16,128,128]{2,1,0:T(8,128)}, u32[]{:S(2)}, u32[]{:S(2)}) collective-permute-start(f32[16,128,128]{2,1,0:T(8,128)S(1)} %reduce_sum.59), channel_id=1, source_target_pairs={{0,8},{8,16},{16,24},{1,9},{9,17},{17,25},{2,10},{10,18},{18,26},{... | collective-permute-start | bytes 3145736 | tf_op jit(solution)/shard_map/ppermute | solution.py:16
  302.4 6.4 %collective-permute-start = (s32[1]{0:T(128)}, s32[1]{0:T(128)}, u32[]{:S(2)}, u32[]{:S(2)}) collective-permute-start(s32[1]{0:T(128)} %select_n.309), channel_id=1, source_target_pairs={{0,8},{8,16},{16,24},{1,9},{9,17},{17,25},{2,10},{10,18},{18,26},{... | collective-permute-start | bytes 20 | tf_op jit(solution)/shard_map/ppermute | solution.py:16
  312.5 39.7 %collective-permute-start.4 = (f32[16,128,128]{2,1,0:T(8,128)}, f32[16,128,128]{2,1,0:T(8,128)}, u32[]{:S(2)}, u32[]{:S(2)}) collective-permute-start(f32[16,128,128]{2,1,0:T(8,128)} %add_select_fusion.5), channel_id=1, source_target_pairs={{0,8},{8,16},{16,24},{1,9},{9,17},{17,25},{2,10},{10,18},{18,26},{... | collective-permute-start | bytes 3145736 | tf_op jit(solution)/shard_map/ppermute | solution.py:16
  343.3 13.1 %copy-start.12 = (pred[512,512]{1,0:T(8,128)(4,1)S(1)}, pred[512,512]{1,0:T(8,128)(4,1)}, u32[]{:S(2)}) copy-start(pred[512,512]{1,0:T(8,128)(4,1)} %fusion.25) | copy-start | bytes 786436
  344.5 6.3 %collective-permute-start.1 = (s32[1]{0:T(128)}, s32[1]{0:T(128)}, u32[]{:S(2)}, u32[]{:S(2)}) collective-permute-start(s32[1]{0:T(128)} %select_n.310), channel_id=1, source_target_pairs={{0,8},{8,16},{16,24},{1,9},{9,17},{17,25},{2,10},{10,18},{18,26},{... | collective-permute-start | bytes 20 | tf_op jit(solution)/shard_map/ppermute | solution.py:16
  354.5 26.0 %collective-permute-start.5 = (f32[16,128,128]{2,1,0:T(8,128)}, f32[16,128,128]{2,1,0:T(8,128)S(1)}, u32[]{:S(2)}, u32[]{:S(2)}) collective-permute-start(f32[16,128,128]{2,1,0:T(8,128)} %add_select_fusion.4), channel_id=1, source_target_pairs={{0,8},{8,16},{16,24},{1,9},{9,17},{17,25},{2,10},{10,18},{18,26},{... | collective-permute-start | bytes 3145736 | tf_op jit(solution)/shard_map/ppermute | solution.py:16
  367.7 11.5 %collective-permute-start.2 = (s32[1]{0:T(128)}, s32[1]{0:T(128)}, u32[]{:S(2)}, u32[]{:S(2)}) collective-permute-start(s32[1]{0:T(128)} %select_n.311), channel_id=1, source_target_pairs={{0,8},{8,16},{16,24},{1,9},{9,17},{17,25},{2,10},{10,18},{18,26},{... | collective-permute-start | bytes 20 | tf_op jit(solution)/shard_map/ppermute | solution.py:16
  380.5 1.9 copy-start.1
  382.4 5.0 %copy-start.3 = (bf16[512,2048]{0,1:T(8,128)(2,1)S(1)}, bf16[512,2048]{0,1:T(8,128)(2,1)}, u32[]{:S(2)}) copy-start(bf16[512,2048]{0,1:T(8,128)(2,1)} %copy.113) | copy-start | bytes 6291460
  382.4 5.0 %copy-start.4 = (f32[16,512,128]{1,2,0:T(8,128)S(1)}, f32[16,512,128]{1,2,0:T(8,128)}, u32[]{:S(2)}) copy-start(f32[16,512,128]{1,2,0:T(8,128)} %fusion.5) | copy-start | bytes 12582916
  387.4 2.6 copy-start
  387.4 2.9 copy-start.2
  390.3 2.7 copy-start.13
Sparse Core Ops, SparseCore 0:
  57.3 83.3 all-gather.8
  192.8 80.4 all-gather.10
